TPU v7x, 32 devices: a whole 2x2x4 slice. The times are simulated.
32 devices in a mesh: groups: 2 (over y), blk: 4 (over z), heads: 2 (over x), sub: 2 (over core).
Axes of the slice: x: 2, y: 2, z: 4, core: 2. Of those that a mesh axis runs over, the one named last changes fastest.
Arguments:
- patches: bfloat16 [1024, 1024], P(('groups', 'blk')), parts along dimension 0, may hold values from -6 to 6
- conv_taps: float32 [3, 1024], replicated, may hold values from -3 to 3
- w_query: bfloat16 [1024, 1024], P(None, ('heads', 'sub')), may hold values from -0.1875 to 0.1875
- w_key: bfloat16 [1024, 1024], P(None, ('heads', 'sub')), may hold values from -0.1875 to 0.1875
- w_value: bfloat16 [1024, 1024], P(None, ('heads', 'sub')), may hold values from -0.1875 to 0.1875
- w_output: bfloat16 [1024, 1024], P(None, ('heads', 'sub')), may hold values from -0.1875 to 0.1875
- tile_mask: int32 [8, 4], P('groups'), parts along dimension 0, may hold values from 0 to 1, as said below
- cotangent: bfloat16 [1024, 1024], P(('groups', 'blk'), ('heads', 'sub')), parts along dimension 0, may hold values from -6 to 6
Outputs:
- input_grad: float32 [1024, 1024], P(('groups', 'blk'), ('heads', 'sub')), parts along dimension 0
- conv_grad: float32 [6, 1024], P('groups', ('heads', 'sub')), parts along dimension 0
- grad_query: float32 [2048, 1024], P(('groups', 'blk'), ('heads', 'sub')), parts along dimension 0
- grad_key: float32 [2048, 1024], P(('groups', 'blk'), ('heads', 'sub')), parts along dimension 0
- grad_value: float32 [2048, 1024], P(('groups', 'blk'), ('heads', 'sub')), parts along dimension 0
- grad_output: float32 [2048, 1024], P(('groups', 'blk'), ('heads', 'sub')), parts along dimension 0
There are 2 independent parts, one for each index of `groups`. A program takes and returns all parts, laid end to end along the dimension named above; an argument that names none is the same for every part. Nothing has to cross between parts.
Inputs may be any that keep to these rules, and one draw needn't show every extreme that they name: tile_mask[i][i] is 1 for every tile and tile_mask is symmetric.
All inputs are finite; a program needn't handle non-finite values.
Results may differ from a plain program's by a relative error of at most 0.004.
The roundings to bfloat16 on the way count: a program that leaves them out, or rounds other values in their place, can miss the bound.
Values may be sent and summed in bfloat16 or wider, within the bound.
A program may use at most 64 MiB of HBM per device.

v0:
```python
import jax
import jax.numpy as jnp
from jax import lax
from jax.sharding import PartitionSpec as P

D = 1024
HEADS = 16
TILE = 128


def padded(cells, sides, width):
    for axis, dim in sides:
        count = lax.axis_size(axis)
        ends = count - 1
        head = lax.slice_in_dim(cells, 0, width, axis=dim)
        tail = lax.slice_in_dim(cells, cells.shape[dim] - width, cells.shape[dim], axis=dim)
        cells = jnp.concatenate(
            [
                lax.ppermute(tail, axis, [(i, (i + 1) % count) for i in range(ends)]),
                cells,
                lax.ppermute(head, axis, [((i + 1) % count, i) for i in range(ends)]),
            ],
            axis=dim,
        )
    return cells


def from_behind(value, axis, steps):
    count = lax.axis_size(axis)
    pairs = [(source, (source + steps) % count) for source in range(count)]
    return lax.ppermute(value, axis, pairs)


def allowed_rows(mask_bf, first_query, query_count, first_key, key_count):
    tiles = mask_bf.shape[0]
    columns = jnp.arange(tiles, dtype=jnp.int32)
    query_tiles = (first_query + jnp.arange(query_count, dtype=jnp.int32)) // TILE
    key_tiles = (first_key + jnp.arange(key_count, dtype=jnp.int32)) // TILE
    query_hot = (query_tiles[:, None] == columns[None, :]).astype(jnp.bfloat16)
    key_hot = (key_tiles[:, None] == columns[None, :]).astype(jnp.bfloat16)
    picked = jnp.dot(query_hot, mask_bf, preferred_element_type=jnp.float32).astype(jnp.bfloat16)
    return jnp.einsum("qn,kn->qk", picked, key_hot, preferred_element_type=jnp.float32) > 0.5


def per_device(patches, conv_taps, w_query, w_key, w_value, w_output, tile_mask, cotangent):
    rows = patches.shape[0]
    local = w_query.shape[1]
    head_size = D // HEADS
    heads_here = local // head_size
    cycle_size = lax.axis_size("blk")
    position = lax.axis_index("blk")
    total_rows = rows * cycle_size
    scale = head_size ** (-0.5)
    norm = total_rows ** (-0.5)
    mask_bf = tile_mask.astype(jnp.bfloat16)
    first_query = position * rows
    padded_in = padded(patches, (("blk", 0),), 1)
    padded32 = padded_in.astype(jnp.float32)
    middle = padded32[1:-1]
    mixed = (
        middle + conv_taps[0] * padded32[:-2] + conv_taps[1] * middle + conv_taps[2] * padded32[2:]
    ).astype(jnp.bfloat16)
    queries = jnp.dot(mixed, w_query, preferred_element_type=jnp.float32).astype(jnp.bfloat16)
    keys_own = jnp.dot(mixed, w_key, preferred_element_type=jnp.float32).astype(jnp.bfloat16)
    values_own = jnp.dot(mixed, w_value, preferred_element_type=jnp.float32).astype(jnp.bfloat16)
    keys_all, values_all = (
        lax.all_gather(keys_own, "blk", axis=0, tiled=True),
        lax.all_gather(values_own, "blk", axis=0, tiled=True),
    )
    cot_full = lax.all_gather(cotangent, ("heads", "sub"), axis=1, tiled=True)
    grad_att = jnp.dot(cot_full, w_output, preferred_element_type=jnp.float32).astype(jnp.bfloat16)
    group = 1
    for power in range(12):
        if group * 2 * rows <= 1024 and cycle_size % (group * 2) == 0:
            group = group * 2
    span = group * rows
    blocks = cycle_size // group
    query_heads = queries.reshape(rows, heads_here, head_size)
    grad_heads = grad_att.reshape(rows, heads_here, head_size)
    key_blocks = keys_all.reshape(blocks, span, heads_here, head_size)
    value_blocks = values_all.reshape(blocks, span, heads_here, head_size)
    block_ids = jnp.arange(blocks, dtype=jnp.int32)

    def weights_of(key_block, allowed):
        raw = (
            jnp.einsum("qhd,khd->hqk", query_heads, key_block, preferred_element_type=jnp.float32)
            * scale
        )
        return jnp.where(allowed[None], jnp.exp(jnp.where(allowed[None], raw, 0.0)), 0.0)

    def forward_step(state, inputs):
        block_id, key_block, value_block = inputs
        allowed = allowed_rows(mask_bf, first_query, rows, block_id * span, span)
        accum, totals = state
        weights = weights_of(key_block, allowed)
        added = jnp.einsum(
            "hqk,khd->hqd",
            weights.astype(jnp.bfloat16),
            value_block,
            preferred_element_type=jnp.float32,
        )
        state = (accum + added, totals + jnp.sum(weights, -1))
        return (state, None)

    start_state = (
        jnp.zeros((heads_here, rows, head_size), jnp.float32),
        jnp.zeros((heads_here, rows), jnp.float32),
    )
    (accum, totals), unused = lax.scan(
        forward_step, start_state, (block_ids, key_blocks, value_blocks)
    )
    attended32 = accum / totals[:, :, None]
    attended = jnp.transpose(attended32, (1, 0, 2)).reshape(rows, local).astype(jnp.bfloat16)
    deltas = jnp.einsum("qhd,hqd->hq", grad_heads.astype(jnp.float32), attended32)

    def local_grads(key_block, value_block, allowed):
        weights = weights_of(key_block, allowed)
        probs = weights / totals[:, :, None]
        dprobs = jnp.einsum(
            "qhd,khd->hqk", grad_heads, value_block, preferred_element_type=jnp.float32
        )
        dscores = (probs * (dprobs - deltas[:, :, None]) * scale).astype(jnp.bfloat16)
        return (
            jnp.einsum("hqk,khd->qhd", dscores, key_block, preferred_element_type=jnp.float32),
            jnp.einsum("hqk,qhd->khd", dscores, query_heads, preferred_element_type=jnp.float32),
            jnp.einsum(
                "hqk,qhd->khd",
                probs.astype(jnp.bfloat16),
                grad_heads,
                preferred_element_type=jnp.float32,
            ),
        )

    def shard_grads(block):
        wrapped = jnp.remainder(block, cycle_size)
        key_block = lax.dynamic_slice_in_dim(keys_all, wrapped * rows, rows, 0).reshape(
            rows, heads_here, head_size
        )
        value_block = lax.dynamic_slice_in_dim(values_all, wrapped * rows, rows, 0).reshape(
            rows, heads_here, head_size
        )
        allowed = allowed_rows(mask_bf, first_query, rows, wrapped * rows, rows)
        query_add, key_term, value_term = local_grads(key_block, value_block, allowed)
        return (
            query_add,
            jnp.stack([key_term.reshape(rows, local), value_term.reshape(rows, local)]),
        )

    query_first, carried_first = shard_grads(position - 1)

    def turn(step, state):
        accum_q, carried = state
        moved = from_behind(carried, "blk", 1)
        query_add, term = shard_grads(position - step - 1)
        return (accum_q + query_add, moved + term)

    accum_q, summed = lax.fori_loop(1, cycle_size, turn, (query_first, carried_first))
    grad_keys = summed[0].astype(jnp.bfloat16)
    grad_values = summed[1].astype(jnp.bfloat16)
    grad_queries = accum_q.reshape(rows, local).astype(jnp.bfloat16)
    stacked = jnp.stack(
        [
            jnp.einsum("td,tc->dc", mixed, grad_queries, preferred_element_type=jnp.float32),
            jnp.einsum("td,tc->dc", mixed, grad_keys, preferred_element_type=jnp.float32),
            jnp.einsum("td,tc->dc", mixed, grad_values, preferred_element_type=jnp.float32),
            jnp.einsum("td,tc->dc", cot_full, attended, preferred_element_type=jnp.float32),
        ]
    )
    weight_sums = lax.psum_scatter(stacked, "blk", scatter_dimension=1, tiled=True) * norm
    partial_grad = (
        jnp.einsum("tc,dc->td", grad_queries, w_query, preferred_element_type=jnp.float32)
        + jnp.einsum("tc,dc->td", grad_keys, w_key, preferred_element_type=jnp.float32)
        + jnp.einsum("tc,dc->td", grad_values, w_value, preferred_element_type=jnp.float32)
    )
    grad_mixed = lax.psum_scatter(
        partial_grad, ("heads", "sub"), scatter_dimension=1, tiled=True
    ) + cotangent.astype(jnp.float32)
    columns_here = cotangent.shape[1]
    offset = lax.axis_index(("heads", "sub")) * columns_here
    taps_here = lax.dynamic_slice_in_dim(conv_taps, offset, columns_here, 1)
    padded_grad = padded(grad_mixed.astype(jnp.bfloat16), (("blk", 0),), 1).astype(grad_mixed.dtype)
    input_grad = (
        grad_mixed * (1.0 + taps_here[1])
        + taps_here[0] * padded_grad[2:]
        + taps_here[2] * padded_grad[:-2]
    )
    patch_cols = lax.dynamic_slice_in_dim(padded32, offset, columns_here, 1)
    conv_terms = jnp.stack(
        [
            jnp.sum(grad_mixed * patch_cols[:-2], 0),
            jnp.sum(grad_mixed * patch_cols[1:-1], 0),
            jnp.sum(grad_mixed * patch_cols[2:], 0),
        ]
    )
    conv_grad = lax.psum(conv_terms, "blk") * norm
    return (input_grad, conv_grad, weight_sums[0], weight_sums[1], weight_sums[2], weight_sums[3])


def solution(mesh):
    in_specs = (
        P(("groups", "blk"), None),
        P(),
        P(None, ("heads", "sub")),
        P(None, ("heads", "sub")),
        P(None, ("heads", "sub")),
        P(None, ("heads", "sub")),
        P("groups", None),
        P(("groups", "blk"), ("heads", "sub")),
    )
    out_specs = (
        P(("groups", "blk"), ("heads", "sub")),
        P("groups", ("heads", "sub")),
        P(("groups", "blk"), ("heads", "sub")),
        P(("groups", "blk"), ("heads", "sub")),
        P(("groups", "blk"), ("heads", "sub")),
        P(("groups", "blk"), ("heads", "sub")),
    )
    return jax.shard_map(
        per_device, mesh=mesh, in_specs=in_specs, out_specs=out_specs, check_vma=False
    )
```

profile of v0, /device:TPU:0, one launch (start us, length us, event | category | flops | bytes accessed | tf_op | source)
XLA Modules:
  0.0 201.9 jit_solution(833007776584470410)
XLA Ops:
  7.2 0.9 fusion.47
  8.1 4.9 %collective-permute-start.1 = (bf16[1,1024]{1,0:T(2,128)(2,1)S(1)}, bf16[1,1024]{1,0:T(2,128)(2,1)S(1)}, u32[]{:S(2)}, u32[]{:S(2)}) collective-permute-start(bf16[1,1024]{1,0:T(2,128)(2,1)S(1)} %get-tuple-element.416), channel_id=1, source_target_pairs={{0,4},{4,8},{8,12},{1,5},{5,9},{9,13},{2,6},{6,10},{10,14},{3,7},{... | collective-permute-start | bytes 6152 | tf_op jit(solution)/shard_map/ppermute | solution.py:19
  13.0 1.3 collective-permute-start.2
  14.4 0.7 convert_element_type.114
  15.1 0.8 fusion.49
  15.9 6.0 %all_gather.10 = bf16[128,1024]{1,0:T(8,128)(2,1)S(1)} all-gather(bf16[128,256]{1,0:T(8,128)(2,1)} %param.17), channel_id=1, replica_groups=mesh['groups'=2,'blk'=4,'heads'=2,'sub'=2] {'heads','sub'}, dimensions={1}, use_global_device_ids=true | all-gather | bytes 327680 | tf_op jit(solution)/shard_map/all_gather | solution.py:70
  22.2 0.3 convolution_compare_fusion.1
  22.5 1.3 convolution_convert_fusion.2
  24.2 1.0 maximum_convert_fusion
  26.3 15.2 %all_gather.9 = bf16[512,256]{1,0:T(8,128)(2,1)S(1)} all-gather(bf16[128,256]{1,0:T(8,128)(2,1)S(1)} %convolution_convert_fusion.4), channel_id=1, replica_groups=mesh['groups'=2,'blk'=4,'heads'=2,'sub'=2] {'blk'}, dimensions={0}, use_global_device_ids=true | all-gather | bytes 327680 | tf_op jit(solution)/shard_map/all_gather | solution.py:67
  41.4 14.4 %all_gather.11 = bf16[512,256]{1,0:T(8,128)(2,1)S(1)} all-gather(bf16[128,256]{1,0:T(8,128)(2,1)S(1)} %convolution_convert_fusion.1), channel_id=1, replica_groups=mesh['groups'=2,'blk'=4,'heads'=2,'sub'=2] {'blk'}, dimensions={0}, use_global_device_ids=true | all-gather | bytes 327680 | tf_op jit(solution)/shard_map/all_gather | solution.py:68
  55.9 0.8 copy.38
  56.7 0.8 copy.41
  57.8 1.5 fusion.50
  59.6 1.9 fusion.37
  62.3 29.1 %while.23 = (s32[]{:T(128)}, f32[128,4,64]{0,2,1:T(8,128)S(1)}, f32[2,128,256]{1,2,0:T(8,128)S(1)}, s32[]{:T(128)}, bf16[512,256]{0,1:T(8,128)(2,1)}, /*index=5*...) while((s32[]{:T(128)}, f32[128,4,64]{0,2,1:T(8,128)S(1)}, ...), condition=%wide.region_2.3_spmd, body=%wide.region_1.2_spmd.sunk | while | flops 42853904 | bytes 4331956 | solution.py:157
  62.3 1.6 collective-permute-start
  64.0 0.3 convolution_compare_fusion.4
  64.5 0.9 constant_dynamic-slice_fusion.6
  65.8 0.3 fusion.126
  66.5 5.7 %collective-permute-done = f32[2,128,256]{1,2,0:T(8,128)S(1)} collective-permute-done((f32[2,128,256]{1,2,0:T(8,128)S(1)}, f32[2,128,256]{1,2,0:T(8,128)S(1)}, u32[]{:S(2)}, u32[]{:S(2)}) %collective-permute-start) | collective-permute-done | bytes 262176 | tf_op jit(solution)/shard_map/while/body/eval_jaxpr/ppermute | solution.py:31
  72.2 1.0 collective-permute-start
  73.2 0.3 convolution_compare_fusion.4
  73.7 0.9 constant_dynamic-slice_fusion.6
  75.0 0.3 fusion.126
  75.6 7.4 %collective-permute-done = f32[2,128,256]{1,2,0:T(8,128)S(1)} collective-permute-done((f32[2,128,256]{1,2,0:T(8,128)S(1)}, f32[2,128,256]{1,2,0:T(8,128)S(1)}, u32[]{:S(2)}, u32[]{:S(2)}) %collective-permute-start) | collective-permute-done | bytes 262176 | tf_op jit(solution)/shard_map/while/body/eval_jaxpr/ppermute | solution.py:31
  83.2 0.3 convolution_compare_fusion.4
  83.7 0.9 constant_dynamic-slice_fusion.6
  85.7 5.7 %collective-permute-done = f32[2,128,256]{1,2,0:T(8,128)S(1)} collective-permute-done((f32[2,128,256]{1,2,0:T(8,128)S(1)}, f32[2,128,256]{1,2,0:T(8,128)S(1)}, u32[]{:S(2)}, u32[]{:S(2)}) %collective-permute-start) | collective-permute-done | bytes 262176 | tf_op jit(solution)/shard_map/while/body/eval_jaxpr/ppermute | solution.py:31
  91.4 0.3 fusion.53
  91.8 0.3 convolution_add_fusion.1
  92.1 1.1 convolution_add_fusion
  93.3 0.3 convolution_bitcast_fusion.4
  93.6 0.3 convolution_bitcast_fusion.2
  93.9 0.3 convolution_bitcast_fusion.3
  94.3 0.3 convolution_bitcast_fusion.1
  94.6 2.2 %pad_maximum_fusion = f32[4,1024,256]{2,1,0:T(8,128)} fusion(f32[1,1024,256]{2,1,0:T(8,128)S(1)} %convolution_bitcast_fusion.1, f32[1,1024,256]{2,1,0:T(8,128)S(1)} %convolution_bitcast_fusion.2, f32[1,1024,256]{2,1,0:T(8,128)S(1)} %convolution_bitcast_fusion.3, f32[1,1024,256]{2,1,0:T(8,128)S(1)} %convolution_bitcast_fusion.4), kind=kLoop, calls=%fused_computation.32 | loop fusion | flops 3145728 | bytes 8388608 | tf_op jit(solution)/shard_map/stack | solution.py:161
  96.9 0.9 dynamic-slice_add_fusion
  97.8 15.5 %reduce-scatter.3.cloned.1.call-done = f32[128,256]{1,0:T(8,128)} async-done(((f32[128,1024]{1,0:T(8,128)}), f32[128,256]{1,0:T(8,128)}) %reduce-scatter.3.cloned.1.call-update) | async-done | bytes 131088 | tf_op jit(solution)/shard_map/reduce_scatter | solution.py:175
  113.3 1.1 fusion.33
  114.3 3.4 %collective-permute-start.3 = (bf16[1,256]{1,0:T(2,128)(2,1)S(1)}, bf16[1,256]{1,0:T(2,128)(2,1)S(1)}, u32[]{:S(2)}, u32[]{:S(2)}) collective-permute-start(bf16[1,256]{1,0:T(2,128)(2,1)S(1)} %get-tuple-element.419), channel_id=1, source_target_pairs={{0,4},{4,8},{8,12},{1,5},{5,9},{9,13},{2,6},{6,10},{10,14},{3,7},{... | collective-permute-start | bytes 1544 | tf_op jit(solution)/shard_map/ppermute | solution.py:19
  117.7 1.3 collective-permute-start.4
  119.1 13.3 %psum.7 = f32[3,256]{1,0:T(4,128)S(1)} all-reduce(f32[3,256]{1,0:T(4,128)S(1)} %pad_maximum_fusion.2), channel_id=1, replica_groups=mesh['groups'=2,'blk'=4,'heads'=2,'sub'=2] {'blk'}, use_global_device_ids=true, to_apply=%region_7.8 | all-reduce | flops 768 | bytes 6144 | tf_op jit(solution)/shard_map/psum | solution.py:195
  132.3 0.6 broadcast_multiply_fusion.1
  133.0 1.6 fusion.34
  134.6 58.2 %reduce-scatter.5.cloned.1.call-done = f32[4,256,256]{2,1,0:T(8,128)} async-done(((f32[4,1024,256]{2,1,0:T(8,128)}), f32[4,256,256]{2,1,0:T(8,128)}) %reduce-scatter.5.cloned.1.call-update) | async-done | bytes 1048592 | tf_op jit(solution)/shard_map/reduce_scatter | solution.py:169
  192.7 1.3 broadcast_multiply_fusion
  194.1 1.0 slice_bitcast_fusion
  (70 shorter events, 6.3 us)
Async XLA Ops:
  7.2 18.5 %copy-start = (bf16[1024,256]{1,0:T(8,128)(2,1)S(1)}, bf16[1024,256]{1,0:T(8,128)(2,1)}, u32[]{:S(2)}) copy-start(bf16[1024,256]{1,0:T(8,128)(2,1)} %param.12) | copy-start | bytes 1572868
  7.2 18.2 %copy-start.2 = (bf16[1024,256]{1,0:T(8,128)(2,1)S(1)}, bf16[1024,256]{1,0:T(8,128)(2,1)}, u32[]{:S(2)}) copy-start(bf16[1024,256]{1,0:T(8,128)(2,1)} %param.14) | copy-start | bytes 1572868
  7.2 18.8 %copy-start.1 = (bf16[1024,256]{1,0:T(8,128)(2,1)S(1)}, bf16[1024,256]{1,0:T(8,128)(2,1)}, u32[]{:S(2)}) copy-start(bf16[1024,256]{1,0:T(8,128)(2,1)} %param.13) | copy-start | bytes 1572868
  7.2 106.1 %reduce-scatter.3.cloned.1.call-start = ((), (), s32[]{:S(2)}) async-start(), calls=%async_computation.2 | async-start | bytes 655360 | tf_op jit(solution)/shard_map/reduce_scatter | solution.py:175
  8.1 16.1 %collective-permute-start.1 = (bf16[1,1024]{1,0:T(2,128)(2,1)S(1)}, bf16[1,1024]{1,0:T(2,128)(2,1)S(1)}, u32[]{:S(2)}, u32[]{:S(2)}) collective-permute-start(bf16[1,1024]{1,0:T(2,128)(2,1)S(1)} %get-tuple-element.416), channel_id=1, source_target_pairs={{0,4},{4,8},{8,12},{1,5},{5,9},{9,13},{2,6},{6,10},{10,14},{3,7},{... | collective-permute-start | bytes 6152 | tf_op jit(solution)/shard_map/ppermute | solution.py:19
  13.0 11.1 %collective-permute-start.2 = (bf16[1,1024]{1,0:T(2,128)(2,1)S(1)}, bf16[1,1024]{1,0:T(2,128)(2,1)S(1)}, u32[]{:S(2)}, u32[]{:S(2)}) collective-permute-start(bf16[1,1024]{1,0:T(2,128)(2,1)S(1)} %get-tuple-element.417), channel_id=1, source_target_pairs={{4,0},{8,4},{12,8},{5,1},{9,5},{13,9},{6,2},{10,6},{14,10},{7,3},{... | collective-permute-start | bytes 6152 | tf_op jit(solution)/shard_map/ppermute | solution.py:21
  62.3 9.8 %collective-permute-start = (f32[2,128,256]{1,2,0:T(8,128)S(1)}, f32[2,128,256]{1,2,0:T(8,128)S(1)}, u32[]{:S(2)}, u32[]{:S(2)}) collective-permute-start(f32[2,128,256]{1,2,0:T(8,128)S(1)} %get-tuple-element.533), channel_id=1, source_target_pairs={{0,4},{4,8},{8,12},{12,0},{1,5},{5,9},{9,13},{13,1},{2,6},{6,10},{... | collective-permute-start | bytes 786440 | tf_op jit(solution)/shard_map/while/body/eval_jaxpr/ppermute | solution.py:31
  72.2 10.9 %collective-permute-start = (f32[2,128,256]{1,2,0:T(8,128)S(1)}, f32[2,128,256]{1,2,0:T(8,128)S(1)}, u32[]{:S(2)}, u32[]{:S(2)}) collective-permute-start(f32[2,128,256]{1,2,0:T(8,128)S(1)} %get-tuple-element.533), channel_id=1, source_target_pairs={{0,4},{4,8},{8,12},{12,0},{1,5},{5,9},{9,13},{13,1},{2,6},{6,10},{... | collective-permute-start | bytes 786440 | tf_op jit(solution)/shard_map/while/body/eval_jaxpr/ppermute | solution.py:31
  83.1 8.2 %collective-permute-start = (f32[2,128,256]{1,2,0:T(8,128)S(1)}, f32[2,128,256]{1,2,0:T(8,128)S(1)}, u32[]{:S(2)}, u32[]{:S(2)}) collective-permute-start(f32[2,128,256]{1,2,0:T(8,128)S(1)} %get-tuple-element.533), channel_id=1, source_target_pairs={{0,4},{4,8},{8,12},{12,0},{1,5},{5,9},{9,13},{13,1},{2,6},{6,10},{... | collective-permute-start | bytes 786440 | tf_op jit(solution)/shard_map/while/body/eval_jaxpr/ppermute | solution.py:31
  91.7 2.5 %copy-start.4 = (f32[4,128,64]{1,2,0:T(8,128)S(1)}, f32[4,128,64]{1,2,0:T(8,128)}, u32[]{:S(2)}) copy-start(f32[4,128,64]{1,2,0:T(8,128)} %get-tuple-element.430) | copy-start | bytes 393220
  93.2 99.5 %reduce-scatter.5.cloned.1.call-start = ((), (), s32[]{:S(2)}) async-start(), calls=%async_computation.3 | async-start | bytes 5242880 | tf_op jit(solution)/shard_map/reduce_scatter | solution.py:169
  96.9 16.4 %copy-start.3 = (bf16[128,256]{1,0:T(8,128)(2,1)S(1)}, bf16[128,256]{1,0:T(8,128)(2,1)}, u32[]{:S(2)}) copy-start(bf16[128,256]{1,0:T(8,128)(2,1)} %param.17) | copy-start | bytes 196612
  114.3 18.6 %collective-permute-start.3 = (bf16[1,256]{1,0:T(2,128)(2,1)S(1)}, bf16[1,256]{1,0:T(2,128)(2,1)S(1)}, u32[]{:S(2)}, u32[]{:S(2)}) collective-permute-start(bf16[1,256]{1,0:T(2,128)(2,1)S(1)} %get-tuple-element.419), channel_id=1, source_target_pairs={{0,4},{4,8},{8,12},{1,5},{5,9},{9,13},{2,6},{6,10},{10,14},{3,7},{... | collective-permute-start | bytes 1544 | tf_op jit(solution)/shard_map/ppermute | solution.py:19
  117.7 15.2 %collective-permute-start.4 = (bf16[1,256]{1,0:T(2,128)(2,1)S(1)}, bf16[1,256]{1,0:T(2,128)(2,1)S(1)}, u32[]{:S(2)}, u32[]{:S(2)}) collective-permute-start(bf16[1,256]{1,0:T(2,128)(2,1)S(1)} %get-tuple-element.420), channel_id=1, source_target_pairs={{4,0},{8,4},{12,8},{5,1},{9,5},{13,9},{6,2},{10,6},{14,10},{7,3},{... | collective-permute-start | bytes 1544 | tf_op jit(solution)/shard_map/ppermute | solution.py:21
Sparse Core Ops, SparseCore 0:
  93.4 19.8 reduce-scatter.2
  115.7 77.0 reduce-scatter.4
where the time goes:
time: 203 us; the launch traced here: 202 us
  waiting for transfers between devices  92.5 us (46%)
  blocking collectives  48.9 us (24%)
  matrix products  14.4 us (7%)
  between operations  14.4 us (7%)
  starting transfers between devices  13.7 us (7%)
  other arithmetic  9.88 us (5%)
  local copies, waits for them, and re-layouts  7.87 us (4%)
    reduce_scatter x1, waiting for transfers between devices, per_device(): lax.psum_scatter(stacked, 'blk', scatter_dimension=1, tiled=True) * norm  58.2 us
    ppermute x3, waiting for transfers between devices, from_behind(): return lax.ppermute(value, axis, pairs)  18.8 us
    reduce_scatter x1, waiting for transfers between devices, per_device(): lax.psum_scatter(partial_grad, ('heads', 'sub'), scatter_dimension=1, til...  15.5 us
    all_gather x1, blocking collectives, per_device(): lax.all_gather(keys_own, 'blk', axis=0, tiled=True)  15.2 us
    all_gather x1, blocking collectives, per_device(): lax.all_gather(values_own, 'blk', axis=0, tiled=True)  14.4 us
    psum x1, blocking collectives, per_device(): conv_grad = lax.psum(conv_terms, 'blk') * norm  13.3 us
    ppermute x2, starting transfers between devices, padded(): lax.ppermute(tail, axis, [(i, (i + 1) % count) for i in range(ends)])  8.32 us
    all_gather x1, blocking collectives, per_device(): cot_full = lax.all_gather(cotangent, ('heads', 'sub'), axis=1, tiled=True)  6 us
  transfers between devices with their start and end apart: 9, of which 5 were waited for; matrix products, arithmetic and copies ran while one was open for 9% of the time, Pallas kernels for 0%

commit v1 on v0

--- a/solution.py
+++ b/solution.py
@@ -1,6 +1,10 @@
+import functools
+
 import jax
 import jax.numpy as jnp
 from jax import lax
+from jax.experimental import pallas as pl
+from jax.experimental.pallas import tpu as pltpu
 from jax.sharding import PartitionSpec as P
 
 D = 1024
@@ -195,6 +199,306 @@
     conv_grad = lax.psum(conv_terms, "blk") * norm
     return (input_grad, conv_grad, weight_sums[0], weight_sums[1], weight_sums[2], weight_sums[3])
 
+MESH = pl.DeviceIdType.MESH
+BF = jnp.bfloat16
+F32 = jnp.float32
+
+
+def dot(a, b, ca, cb):
+    return lax.dot_general(a, b, (((ca,), (cb,)), ((), ())), preferred_element_type=F32)
+
+
+def fused(
+    n, norm,
+    patches, taps, w_query, w_key, w_value, w_output, mask, cot,
+    out_in, out_conv, out_q, out_k, out_v, out_o,
+    slabs, mixed, wq, wk, wv, wo, tp, acc, heads4, grads, att, acc_k, acc_v,
+    back_out, back_in, wide_out, wide_in, part_out, part_in, edge_out, edge_in,
+    sem_loc, sem_w, zs, zr, xs, xr, cs, cr, bs, br, gs, gr, ps, pr, es, er,
+):
+    g = lax.axis_index("groups")
+    b = lax.axis_index("blk")
+    x = lax.axis_index("heads")
+    s = lax.axis_index("sub")
+    h, hx, hc, hd = x * 2 + s, (1 - x) * 2 + s, x * 2 + 1 - s, (1 - x) * 2 + 1 - s
+    rows = patches.shape[0]
+    wide = cot.shape[1]
+    half = wide // 2
+    hs = D // HEADS
+    scale = hs ** (-0.5)
+    peers = [lax.rem(b + k, n) for k in range(1, n)]
+    at_peer = [(g, p, x, s) for p in peers]
+    at_x, at_c, at_d = (g, b, 1 - x, s), (g, b, x, 1 - s), (g, b, 1 - x, 1 - s)
+
+    def send(src, dst, ss, rs, where):
+        c = pltpu.make_async_remote_copy(
+            src_ref=src, dst_ref=dst, send_sem=ss, recv_sem=rs, device_id=where, device_id_type=MESH
+        )
+        c.start()
+        return c
+
+    def got(ref, sem):
+        pltpu.make_async_remote_copy(
+            src_ref=ref, dst_ref=ref, send_sem=sem, recv_sem=sem, device_id=at_x, device_id_type=MESH
+        ).wait_recv()
+
+    locals_ = []
+    for c in range(4):
+        locals_.append(
+            pltpu.make_async_copy(
+                patches.at[:, pl.ds(c * wide, wide)], slabs.at[b, c, 0], sem_loc.at[c]
+            )
+        )
+    locals_.append(pltpu.make_async_copy(cot, slabs.at[b, h, 1], sem_loc.at[4]))
+    locals_.append(pltpu.make_async_copy(taps, tp, sem_loc.at[5]))
+    weights = [
+        pltpu.make_async_copy(src, dst, sem_w.at[i])
+        for i, (src, dst) in enumerate(((w_query, wq), (w_key, wk), (w_value, wv), (w_output, wo)))
+    ]
+    for c in locals_ + weights:
+        c.start()
+    barrier = pltpu.get_barrier_semaphore()
+    for where in at_peer + [at_x, at_c, at_d]:
+        pl.semaphore_signal(barrier, inc=1, device_id=where, device_id_type=MESH)
+    pl.semaphore_wait(barrier, n + 2)
+
+    sent = []
+    own_cols = pl.ds(pl.multiple_of(h * wide, wide), wide)
+    for k, where in enumerate(at_peer):
+        sent.append(send(patches.at[:, own_cols], slabs.at[b, h, 0], zs.at[0, k], zr.at[0, b], where))
+        sent.append(send(cot, slabs.at[b, h, 1], zs.at[1, k], zr.at[1, b], where))
+    sent.append(send(cot, slabs.at[b, h, 1], xs.at[0], xr.at[b], at_x))
+    sent.append(send(cot, slabs.at[b, h, 1], cs.at[0, 0], cr.at[0, b], at_c))
+    for k, p in enumerate(peers):
+        got(slabs.at[p, h, 0], zr.at[0, p])
+        got(slabs.at[p, h, 1], zr.at[1, p])
+        sent.append(send(slabs.at[p, h], slabs.at[p, h], xs.at[k + 1], xr.at[p], at_x))
+        sent.append(send(slabs.at[p, h], slabs.at[p, h], cs.at[0, k + 1], cr.at[0, p], at_c))
+    for c in locals_ + weights:
+        c.wait()
+
+    pair = pl.ds(pl.multiple_of((b // 2) * half, half), half)
+    acc[...] = jnp.zeros_like(acc)
+    row_of = lax.broadcasted_iota(jnp.int32, (n * rows, wide), 0)
+
+    def quarter(c):
+        cols = pl.ds(pl.multiple_of(c * wide, wide), wide)
+        plain = slabs[:, c, 0].reshape(n * rows, wide).astype(F32)
+        before = jnp.where(row_of == 0, 0.0, pltpu.roll(plain, 1, 0))
+        after = jnp.where(row_of == n * rows - 1, 0.0, pltpu.roll(plain, n * rows - 1, 0))
+        t = tp[:, cols]
+        m = (plain + t[0:1] * before + t[1:2] * plain + t[2:3] * after).astype(BF)
+        mixed[c] = m
+        cq = slabs[:, c, 1].reshape(n * rows, wide)
+        acc[0] += dot(m, wq[cols, pair], 1, 0)
+        acc[1] += dot(m, wk[cols, pair], 1, 0)
+        acc[2] += dot(m, wv[cols, pair], 1, 0)
+        acc[3] += dot(cq, wo[cols, pair], 1, 0)
+
+    quarter(h)
+    got(slabs.at[b, hx, 1], xr.at[b])
+    sent.append(send(slabs.at[b, hx, 1], slabs.at[b, hx, 1], cs.at[1, 0], cr.at[1, b], at_c))
+    for k, p in enumerate(peers):
+        got(slabs.at[p, hx], xr.at[p])
+        sent.append(send(slabs.at[p, hx], slabs.at[p, hx], cs.at[1, k + 1], cr.at[1, p], at_c))
+    quarter(hx)
+    got(slabs.at[b, hc, 1], cr.at[0, b])
+    for p in peers:
+        got(slabs.at[p, hc], cr.at[0, p])
+    quarter(hc)
+    got(slabs.at[b, hd, 1], cr.at[1, b])
+    for p in peers:
+        got(slabs.at[p, hd], cr.at[1, p])
+    quarter(hd)
+
+    odd = lax.rem(b, 2) == 1
+    for i in range(4):
+        full = acc[i]
+        heads4[i] = jnp.where(odd, pltpu.roll(full, hs, 1), full)[:, :hs].astype(BF)
+
+    acc_k[...] = jnp.zeros_like(acc_k)
+    acc_v[...] = jnp.zeros_like(acc_v)
+    keys, values = heads4[1], heads4[2]
+    for i in range(n):
+        here = pl.ds(i * rows, rows)
+        query, grad = heads4[0, here, :], heads4[3, here, :]
+        allowed = (
+            jnp.concatenate([jnp.full((rows, TILE), mask[i, j], jnp.int32) for j in range(n)], axis=1)
+            == 1
+        )
+        score = dot(query, keys, 1, 1) * scale
+        weight = jnp.where(allowed, jnp.exp(jnp.where(allowed, score, 0.0)), 0.0)
+        inverse = 1.0 / jnp.sum(weight, -1, keepdims=True)
+        att32 = dot(weight.astype(BF), values, 1, 0) * inverse
+        delta = jnp.sum(grad.astype(F32) * att32, -1, keepdims=True)
+        prob = weight * inverse
+        dprob = dot(grad, values, 1, 1)
+        dscore = (prob * (dprob - delta) * scale).astype(BF)
+        att[here, :] = att32.astype(BF)
+        grads[here, 0:hs] = dot(dscore, keys, 1, 0).astype(BF)
+        acc_k[...] += dot(dscore, query, 0, 0)
+        acc_v[...] += dot(prob.astype(BF), grad, 0, 0)
+    grads[:, hs : 2 * hs] = acc_k[...].astype(BF)
+    grads[:, 2 * hs : 3 * hs] = acc_v[...].astype(BF)
+
+    def packed(t):
+        base = pl.multiple_of(t * rows, rows)
+        both = grads[pl.ds(base, rows), 0 : 2 * hs]
+        third = grads[pl.ds(base, rows), 2 * hs : 3 * hs]
+        return both, jnp.concatenate([third[: rows // 2], third[rows // 2 :]], axis=1)
+
+    for k, p in enumerate(peers):
+        both, third = packed(p)
+        back_out[k, :rows] = both
+        back_out[k, rows:] = third
+        sent.append(send(back_out.at[k], back_in.at[b], bs.at[k], br.at[b], at_peer[k]))
+    both, third = packed(b)
+    back_in[b, :rows] = both
+    back_in[b, rows:] = third
+
+    three = grads[...]
+    attended = att[...]
+
+    def weight_grads(c):
+        m = dot(mixed[c], three, 0, 0) * norm
+        o = dot(slabs[:, c, 1].reshape(n * rows, wide), attended, 0, 0) * norm
+        first = m[:, : 2 * hs].astype(BF)
+        return first, jnp.concatenate([m[:, 2 * hs :], o], axis=1).astype(BF)
+
+    for k, p in enumerate(peers):
+        first, second = weight_grads(p)
+        wide_out[k, 0] = first
+        wide_out[k, 1] = second
+        sent.append(send(wide_out.at[k], wide_in.at[b], gs.at[k], gr.at[b], at_peer[k]))
+    first, second = weight_grads(b)
+    wide_in[b, 0] = first
+    wide_in[b, 1] = second
+
+    for p in peers:
+        got(back_in.at[p], br.at[p])
+    grad_q = jnp.concatenate([back_in[j, :rows, :hs] for j in range(n)], axis=1)
+    grad_k = jnp.concatenate([back_in[j, :rows, hs:] for j in range(n)], axis=1)
+    grad_v = jnp.concatenate(
+        [
+            jnp.concatenate([back_in[j, rows:, :hs] for j in range(n)], axis=1),
+            jnp.concatenate([back_in[j, rows:, hs:] for j in range(n)], axis=1),
+        ],
+        axis=0,
+    )
+
+    def branch(c):
+        cols = pl.ds(pl.multiple_of(c * wide, wide), wide)
+        return (
+            dot(grad_q, wq[cols, :], 1, 1) + dot(grad_k, wk[cols, :], 1, 1)
+            + dot(grad_v, wv[cols, :], 1, 1)
+        )
+
+    for k, (c, where) in enumerate(((hx, at_x), (hd, at_d), (hc, at_c))):
+        part_out[k] = branch(c).astype(BF)
+        sent.append(send(part_out.at[k], part_in.at[k], ps.at[k], pr.at[k], where))
+    total = branch(h) + slabs[b, h, 1].astype(F32)
+    for k in range(3):
+        got(part_in.at[k], pr.at[k])
+        total = total + part_in[k].astype(F32)
+
+    first_row = lax.broadcasted_iota(jnp.int32, (rows, wide), 0) == 0
+    last_row = lax.broadcasted_iota(jnp.int32, (rows, wide), 0) == rows - 1
+    low, high = lax.rem(b + n - 1, n), lax.rem(b + 1, n)
+    plain = slabs[b, h, 0].astype(F32)
+    edge_low = jnp.where(b > 0, slabs[low, h, 0, rows - 16 :].astype(F32)[15:16], 0.0)
+    edge_high = jnp.where(b < n - 1, slabs[high, h, 0, :16].astype(F32)[0:1], 0.0)
+    before = jnp.where(first_row, edge_low, pltpu.roll(plain, 1, 0))
+    after = jnp.where(last_row, edge_high, pltpu.roll(plain, rows - 1, 0))
+    edge_out[0:1] = jnp.sum(total * before, 0, keepdims=True)
+    edge_out[1:2] = jnp.sum(total * plain, 0, keepdims=True)
+    edge_out[2:3] = jnp.sum(total * after, 0, keepdims=True)
+    edge_out[3:4] = total[0:1]
+    edge_out[4:5] = total[rows - 1 :]
+    edge_out[5:8] = jnp.zeros((3, wide), F32)
+    for k, where in enumerate(at_peer):
+        sent.append(send(edge_out, edge_in.at[b], es.at[k], er.at[b], where))
+    edge_in[b] = edge_out[...]
+
+    for p in peers:
+        got(wide_in.at[p], gr.at[p])
+    for slot, side, out in ((0, 0, out_q), (0, 1, out_k), (1, 0, out_v), (1, 1, out_o)):
+        out[...] = jnp.concatenate(
+            [wide_in[j, slot, :, side * hs : (side + 1) * hs] for j in range(n)], axis=1
+        ).astype(F32)
+    for p in peers:
+        got(edge_in.at[p], er.at[p])
+    summed = edge_in[0]
+    for j in range(1, n):
+        summed = summed + edge_in[j]
+    out_conv[...] = summed[0:3] * norm
+    t = tp[:, own_cols]
+    edge_low = jnp.where(b > 0, edge_in[low][4:5], 0.0)
+    edge_high = jnp.where(b < n - 1, edge_in[high][3:4], 0.0)
+    before = jnp.where(first_row, edge_low, pltpu.roll(total, 1, 0))
+    after = jnp.where(last_row, edge_high, pltpu.roll(total, rows - 1, 0))
+    out_in[...] = total * (1.0 + t[1:2]) + t[0:1] * after + t[2:3] * before
+    for c in sent:
+        c.wait_send()
+
+
+def fused_device(patches, conv_taps, w_query, w_key, w_value, w_output, tile_mask, cotangent):
+    n = lax.axis_size("blk")
+    rows, wide = cotangent.shape
+    hs = D // HEADS
+    tokens = n * rows
+    dma = pltpu.SemaphoreType.DMA
+    anywhere = pl.BlockSpec(memory_space=pl.ANY)
+    return pl.pallas_call(
+        functools.partial(fused, n, tokens ** (-0.5)),
+        out_shape=(
+            jax.ShapeDtypeStruct((rows, wide), F32),
+            jax.ShapeDtypeStruct((3, wide), F32),
+        )
+        + (jax.ShapeDtypeStruct((D // n, wide), F32),) * 4,
+        in_specs=[anywhere] * 6 + [pl.BlockSpec(memory_space=pltpu.SMEM), anywhere],
+        out_specs=(pl.BlockSpec(memory_space=pltpu.VMEM),) * 6,
+        scratch_shapes=[
+            pltpu.VMEM((n, 4, 2, rows, wide), BF),
+            pltpu.VMEM((4, tokens, wide), BF),
+            pltpu.VMEM((D, wide), BF),
+            pltpu.VMEM((D, wide), BF),
+            pltpu.VMEM((D, wide), BF),
+            pltpu.VMEM((D, wide), BF),
+            pltpu.VMEM((3, D), F32),
+            pltpu.VMEM((4, tokens, wide // 2), F32),
+            pltpu.VMEM((4, tokens, hs), BF),
+            pltpu.VMEM((tokens, 3 * hs), BF),
+            pltpu.VMEM((tokens, hs), BF),
+            pltpu.VMEM((tokens, hs), F32),
+            pltpu.VMEM((tokens, hs), F32),
+            pltpu.VMEM((n - 1, rows + rows // 2, 2 * hs), BF),
+            pltpu.VMEM((n, rows + rows // 2, 2 * hs), BF),
+            pltpu.VMEM((n - 1, 2, D // n, 2 * hs), BF),
+            pltpu.VMEM((n, 2, D // n, 2 * hs), BF),
+            pltpu.VMEM((3, rows, wide), BF),
+            pltpu.VMEM((3, rows, wide), BF),
+            pltpu.VMEM((8, wide), F32),
+            pltpu.VMEM((n, 8, wide), F32),
+            dma((6,)), dma((4,)),
+            dma((2, n - 1)), dma((2, n)),
+            dma((n,)), dma((n,)),
+            dma((2, n)), dma((2, n)),
+            dma((n - 1,)), dma((n,)),
+            dma((n - 1,)), dma((n,)),
+            dma((3,)), dma((3,)),
+            dma((n - 1,)), dma((n,)),
+        ],
+        compiler_params=pltpu.CompilerParams(
+            collective_id=0, has_side_effects=True, vmem_limit_bytes=48 * 1024 * 1024
+        ),
+    )(patches, conv_taps, w_query, w_key, w_value, w_output, tile_mask, cotangent)
+
+
+def fits(mesh):
+    shape = mesh.shape
+    n = shape["blk"]
+    return n == 4 and shape["heads"] == 2 and shape["sub"] == 2 and HEADS == 4 * n
+
 
 def solution(mesh):
     in_specs = (
@@ -216,5 +520,5 @@
         P(("groups", "blk"), ("heads", "sub")),
     )
     return jax.shard_map(
-        per_device, mesh=mesh, in_specs=in_specs, out_specs=out_specs, check_vma=False
-    )
+        fused_device if fits(mesh) else per_device, mesh=mesh, in_specs=in_specs, out_specs=out_specs, check_vma=False
+    )

time: 203 us -> 63.6 us (0.31)
  waiting for transfers between devices: 92.5 us -> 0 us
  Pallas kernels: 0 us -> 51 us
  blocking collectives: 48.9 us -> 0 us
  matrix products: 14.4 us -> 0 us
  between operations: 14.4 us -> 0.66 us
  starting transfers between devices: 13.7 us -> 0 us
  other arithmetic: 9.88 us -> 0 us
  local copies, waits for them, and re-layouts: 7.87 us -> 11.4 us
    reduce_scatter x2 -> x0, waiting for transfers between devices: 73.7 us -> none  [the longest x1 58.2 us: per_device(): lax.psum_scatter(stacked, 'blk', scatter_dimension=1, tiled=True) * norm]
    pallas_call x0 -> x1, Pallas kernels: none -> 51 us  [fused_device(): pl.pallas_call(functools.partial(fused, n, tokens ** (-0.5)), out_shape=(...]
    all_gather x3 -> x0, blocking collectives: 35.6 us -> none  [the longest x1 15.2 us: per_device(): lax.all_gather(keys_own, 'blk', axis=0, tiled=True)]
    ppermute x7 -> x0, waiting for transfers between devices: 18.8 us -> none  [the longest x3 18.8 us: from_behind(): return lax.ppermute(value, axis, pairs)]
    dot_general x39 -> x0, matrix products: 14.4 us -> none  [the longest x5 2.56 us: weights_of(): jnp.einsum('qhd,khd->hqk', query_heads, key_block, preferred_element_type...]
    ppermute x7 -> x0, starting transfers between devices: 13.6 us -> none  [the longest x2 8.32 us: padded(): lax.ppermute(tail, axis, [(i, (i + 1) % count) for i in range(ends)])]
    psum x1 -> x0, blocking collectives: 13.3 us -> none  [per_device(): conv_grad = lax.psum(conv_terms, 'blk') * norm]
    unnamed x10 -> x22, local copies, waits for them, and re-layouts: 0.03 us -> 11.4 us
  transfers between devices with their start and end apart: 9 -> 0, of which waited for: 5 -> 0; matrix products, arithmetic and copies ran while one was open for 9% -> 0% of each run, Pallas kernels for 0% -> 0%
where the time goes in v1:
time: 63.6 us; the launch traced here: 63.1 us
  Pallas kernels  51 us (80%)
  local copies, waits for them, and re-layouts  11.4 us (18%)
  between operations  0.66 us (1%)
    pallas_call x1, Pallas kernels, fused_device(): pl.pallas_call(functools.partial(fused, n, tokens ** (-0.5)), out_shape=(...  51 us
    unnamed x22, local copies, waits for them, and re-layouts  11.4 us

profile of v1, /device:TPU:0, one launch (start us, length us, event | category | flops | bytes accessed | tf_op | source)
XLA Modules:
  0.0 63.1 jit_solution(5115561020370431395)
XLA Ops:
  0.6 0.0 copy-start
  0.6 1.0 %copy-done = bf16[1024,256]{1,0:T(8,128)(2,1)S(1)} copy-done((bf16[1024,256]{1,0:T(8,128)(2,1)S(1)}, bf16[1024,256]{1,0:T(8,128)(2,1)}, u32[]{:S(2)}) %copy-start) | copy-done | bytes 524312
  1.7 0.0 copy-start.1
  1.7 1.0 %copy-done.1 = bf16[1024,256]{1,0:T(8,128)(2,1)S(1)} copy-done((bf16[1024,256]{1,0:T(8,128)(2,1)S(1)}, bf16[1024,256]{1,0:T(8,128)(2,1)}, u32[]{:S(2)}) %copy-start.1) | copy-done | bytes 524312
  2.7 0.0 copy-start.2
  2.7 1.0 %copy-done.2 = bf16[1024,256]{1,0:T(8,128)(2,1)S(1)} copy-done((bf16[1024,256]{1,0:T(8,128)(2,1)S(1)}, bf16[1024,256]{1,0:T(8,128)(2,1)}, u32[]{:S(2)}) %copy-start.2) | copy-done | bytes 524312
  3.8 0.0 copy-start.3
  3.8 1.0 %copy-done.3 = bf16[1024,256]{1,0:T(8,128)(2,1)S(1)} copy-done((bf16[1024,256]{1,0:T(8,128)(2,1)S(1)}, bf16[1024,256]{1,0:T(8,128)(2,1)}, u32[]{:S(2)}) %copy-start.3) | copy-done | bytes 524312
  4.8 0.0 copy-start.4
  4.8 0.9 %copy-done.4 = bf16[128,1024]{1,0:T(8,128)(2,1)S(1)} copy-done((bf16[128,1024]{1,0:T(8,128)(2,1)S(1)}, bf16[128,1024]{1,0:T(8,128)(2,1)}, u32[]{:S(2)}) %copy-start.4) | copy-done | bytes 262168
  5.8 0.0 copy-start.5
  5.8 0.8 %copy-done.5 = bf16[128,256]{1,0:T(8,128)(2,1)S(1)} copy-done((bf16[128,256]{1,0:T(8,128)(2,1)S(1)}, bf16[128,256]{1,0:T(8,128)(2,1)}, u32[]{:S(2)}) %copy-start.5) | copy-done | bytes 65560
  6.6 0.0 copy-start.6
  6.6 0.7 %copy-done.6 = f32[3,1024]{1,0:T(4,128)S(1)} copy-done((f32[3,1024]{1,0:T(4,128)S(1)}, f32[3,1024]{1,0:T(4,128)}, u32[]{:S(2)}) %copy-start.6) | copy-done | bytes 12312
  7.3 0.0 copy-start.7
  7.3 0.7 %copy-done.7 = s32[4,4]{1,0:T(4,128)S(1)} copy-done((s32[4,4]{1,0:T(4,128)S(1)}, s32[4,4]{1,0:T(4,128)}, u32[]{:S(2)}) %copy-start.7) | copy-done | bytes 88
  8.0 51.0 %shard_map.127 = (f32[128,256]{1,0:T(8,128)S(1)}, f32[3,256]{1,0:T(4,128)S(1)}, f32[256,256]{1,0:T(8,128)S(1)}, f32[256,256]{1,0:T(8,128)S(1)}, f32[256,256]{1,0:T(8,128)S(1)}, /*index=5*/f32[256,256]{1,0:T(8,128)S(1)}) custom-call(bf16[128,1024]{1,0:T(8,128)(2,1)S(1)} %copy-done.4, f32[3,1024]{1,0:T(4,128)S(1)} %copy-done.6, bf16[1024,256]{1,0:T(8,128)(2,1)S(1)} %copy-done, ...), custom_call_target="tpu_custom_call" | custom-call | tf_op jit(solution)/shard_map/pallas_call | solution.py:451
  59.0 0.7 %copy.20 = f32[128,256]{1,0:T(8,128)} copy(f32[128,256]{1,0:T(8,128)S(1)} %get-tuple-element.12) | data formatting | bytes 262144
  59.7 0.6 copy.21
  60.3 0.7 %copy.22 = f32[256,256]{1,0:T(8,128)} copy(f32[256,256]{1,0:T(8,128)S(1)} %get-tuple-element.14) | data formatting | bytes 524288
  61.0 0.7 %copy.23 = f32[256,256]{1,0:T(8,128)} copy(f32[256,256]{1,0:T(8,128)S(1)} %get-tuple-element.15) | data formatting | bytes 524288
  61.7 0.7 %copy.24 = f32[256,256]{1,0:T(8,128)} copy(f32[256,256]{1,0:T(8,128)S(1)} %get-tuple-element.16) | data formatting | bytes 524288
  62.4 0.7 %copy.25 = f32[256,256]{1,0:T(8,128)} copy(f32[256,256]{1,0:T(8,128)S(1)} %get-tuple-element.17) | data formatting | bytes 524288
Async XLA Ops:
  0.6 1.0 %copy-start = (bf16[1024,256]{1,0:T(8,128)(2,1)S(1)}, bf16[1024,256]{1,0:T(8,128)(2,1)}, u32[]{:S(2)}) copy-start(bf16[1024,256]{1,0:T(8,128)(2,1)} %w_query.1) | copy-start | bytes 1572868
  1.7 1.0 %copy-start.1 = (bf16[1024,256]{1,0:T(8,128)(2,1)S(1)}, bf16[1024,256]{1,0:T(8,128)(2,1)}, u32[]{:S(2)}) copy-start(bf16[1024,256]{1,0:T(8,128)(2,1)} %w_key.1) | copy-start | bytes 1572868
  2.7 1.0 %copy-start.2 = (bf16[1024,256]{1,0:T(8,128)(2,1)S(1)}, bf16[1024,256]{1,0:T(8,128)(2,1)}, u32[]{:S(2)}) copy-start(bf16[1024,256]{1,0:T(8,128)(2,1)} %w_value.1) | copy-start | bytes 1572868
  3.8 1.0 %copy-start.3 = (bf16[1024,256]{1,0:T(8,128)(2,1)S(1)}, bf16[1024,256]{1,0:T(8,128)(2,1)}, u32[]{:S(2)}) copy-start(bf16[1024,256]{1,0:T(8,128)(2,1)} %w_output.1) | copy-start | bytes 1572868
  4.8 0.9 %copy-start.4 = (bf16[128,1024]{1,0:T(8,128)(2,1)S(1)}, bf16[128,1024]{1,0:T(8,128)(2,1)}, u32[]{:S(2)}) copy-start(bf16[128,1024]{1,0:T(8,128)(2,1)} %patches.1) | copy-start | bytes 786436
  5.8 0.8 %copy-start.5 = (bf16[128,256]{1,0:T(8,128)(2,1)S(1)}, bf16[128,256]{1,0:T(8,128)(2,1)}, u32[]{:S(2)}) copy-start(bf16[128,256]{1,0:T(8,128)(2,1)} %cot.1) | copy-start | bytes 196612
  6.6 0.7 %copy-start.6 = (f32[3,1024]{1,0:T(4,128)S(1)}, f32[3,1024]{1,0:T(4,128)}, u32[]{:S(2)}) copy-start(f32[3,1024]{1,0:T(4,128)} %taps.1) | copy-start | bytes 36868
  7.3 0.7 %copy-start.7 = (s32[4,4]{1,0:T(4,128)S(1)}, s32[4,4]{1,0:T(4,128)}, u32[]{:S(2)}) copy-start(s32[4,4]{1,0:T(4,128)} %mask.1) | copy-start | bytes 196

commit v2 on v1

--- a/solution.py
+++ b/solution.py
@@ -210,11 +210,11 @@
 
 def fused(
     n, norm,
-    patches, taps, w_query, w_key, w_value, w_output, mask, cot,
+    patches, taps, w_query, w_key, w_value, w_output, mask_in, cot,
     out_in, out_conv, out_q, out_k, out_v, out_o,
-    slabs, mixed, wq, wk, wv, wo, tp, acc, heads4, grads, att, acc_k, acc_v,
-    back_out, back_in, wide_out, wide_in, part_out, part_in, edge_out, edge_in,
-    sem_loc, sem_w, zs, zr, xs, xr, cs, cr, bs, br, gs, gr, ps, pr, es, er,
+    mask, slabs, mixed, wq, wk, wv, wo, tp, acc, heads4, grads, probs, dscores, held,
+    part_out, part_in, edge_out, edge_in,
+    sem_loc, sem_w, zs, zr, xs, xr, cs, cr, ps, pr, es, er,
 ):
     g = lax.axis_index("groups")
     b = lax.axis_index("blk")
@@ -223,7 +223,7 @@
     h, hx, hc, hd = x * 2 + s, (1 - x) * 2 + s, x * 2 + 1 - s, (1 - x) * 2 + 1 - s
     rows = patches.shape[0]
     wide = cot.shape[1]
-    half = wide // 2
+    local = wide // (D // HEADS)
     hs = D // HEADS
     scale = hs ** (-0.5)
     peers = [lax.rem(b + k, n) for k in range(1, n)]
@@ -251,6 +251,7 @@
         )
     locals_.append(pltpu.make_async_copy(cot, slabs.at[b, h, 1], sem_loc.at[4]))
     locals_.append(pltpu.make_async_copy(taps, tp, sem_loc.at[5]))
+    locals_.append(pltpu.make_async_copy(mask_in, mask, sem_loc.at[6]))
     weights = [
         pltpu.make_async_copy(src, dst, sem_w.at[i])
         for i, (src, dst) in enumerate(((w_query, wq), (w_key, wk), (w_value, wv), (w_output, wo)))
@@ -277,7 +278,6 @@
     for c in locals_ + weights:
         c.wait()
 
-    pair = pl.ds(pl.multiple_of((b // 2) * half, half), half)
     acc[...] = jnp.zeros_like(acc)
     row_of = lax.broadcasted_iota(jnp.int32, (n * rows, wide), 0)
 
@@ -290,10 +290,10 @@
         m = (plain + t[0:1] * before + t[1:2] * plain + t[2:3] * after).astype(BF)
         mixed[c] = m
         cq = slabs[:, c, 1].reshape(n * rows, wide)
-        acc[0] += dot(m, wq[cols, pair], 1, 0)
-        acc[1] += dot(m, wk[cols, pair], 1, 0)
-        acc[2] += dot(m, wv[cols, pair], 1, 0)
-        acc[3] += dot(cq, wo[cols, pair], 1, 0)
+        acc[0] += dot(m, wq[cols, :], 1, 0)
+        acc[1] += dot(m, wk[cols, :], 1, 0)
+        acc[2] += dot(m, wv[cols, :], 1, 0)
+        acc[3] += dot(cq, wo[cols, :], 1, 0)
 
     quarter(h)
     got(slabs.at[b, hx, 1], xr.at[b])
@@ -311,80 +311,43 @@
         got(slabs.at[p, hd], cr.at[1, p])
     quarter(hd)
 
-    odd = lax.rem(b, 2) == 1
     for i in range(4):
-        full = acc[i]
-        heads4[i] = jnp.where(odd, pltpu.roll(full, hs, 1), full)[:, :hs].astype(BF)
-
-    acc_k[...] = jnp.zeros_like(acc_k)
-    acc_v[...] = jnp.zeros_like(acc_v)
-    keys, values = heads4[1], heads4[2]
-    for i in range(n):
-        here = pl.ds(i * rows, rows)
-        query, grad = heads4[0, here, :], heads4[3, here, :]
-        allowed = (
-            jnp.concatenate([jnp.full((rows, TILE), mask[i, j], jnp.int32) for j in range(n)], axis=1)
-            == 1
-        )
-        score = dot(query, keys, 1, 1) * scale
-        weight = jnp.where(allowed, jnp.exp(jnp.where(allowed, score, 0.0)), 0.0)
-        inverse = 1.0 / jnp.sum(weight, -1, keepdims=True)
-        att32 = dot(weight.astype(BF), values, 1, 0) * inverse
-        delta = jnp.sum(grad.astype(F32) * att32, -1, keepdims=True)
-        prob = weight * inverse
-        dprob = dot(grad, values, 1, 1)
-        dscore = (prob * (dprob - delta) * scale).astype(BF)
-        att[here, :] = att32.astype(BF)
-        grads[here, 0:hs] = dot(dscore, keys, 1, 0).astype(BF)
-        acc_k[...] += dot(dscore, query, 0, 0)
-        acc_v[...] += dot(prob.astype(BF), grad, 0, 0)
-    grads[:, hs : 2 * hs] = acc_k[...].astype(BF)
-    grads[:, 2 * hs : 3 * hs] = acc_v[...].astype(BF)
-
-    def packed(t):
-        base = pl.multiple_of(t * rows, rows)
-        both = grads[pl.ds(base, rows), 0 : 2 * hs]
-        third = grads[pl.ds(base, rows), 2 * hs : 3 * hs]
-        return both, jnp.concatenate([third[: rows // 2], third[rows // 2 :]], axis=1)
-
-    for k, p in enumerate(peers):
-        both, third = packed(p)
-        back_out[k, :rows] = both
-        back_out[k, rows:] = third
-        sent.append(send(back_out.at[k], back_in.at[b], bs.at[k], br.at[b], at_peer[k]))
-    both, third = packed(b)
-    back_in[b, :rows] = both
-    back_in[b, rows:] = third
-
-    three = grads[...]
-    attended = att[...]
-
-    def weight_grads(c):
-        m = dot(mixed[c], three, 0, 0) * norm
-        o = dot(slabs[:, c, 1].reshape(n * rows, wide), attended, 0, 0) * norm
-        first = m[:, : 2 * hs].astype(BF)
-        return first, jnp.concatenate([m[:, 2 * hs :], o], axis=1).astype(BF)
-
-    for k, p in enumerate(peers):
-        first, second = weight_grads(p)
-        wide_out[k, 0] = first
-        wide_out[k, 1] = second
-        sent.append(send(wide_out.at[k], wide_in.at[b], gs.at[k], gr.at[b], at_peer[k]))
-    first, second = weight_grads(b)
-    wide_in[b, 0] = first
-    wide_in[b, 1] = second
-
-    for p in peers:
-        got(back_in.at[p], br.at[p])
-    grad_q = jnp.concatenate([back_in[j, :rows, :hs] for j in range(n)], axis=1)
-    grad_k = jnp.concatenate([back_in[j, :rows, hs:] for j in range(n)], axis=1)
-    grad_v = jnp.concatenate(
-        [
-            jnp.concatenate([back_in[j, rows:, :hs] for j in range(n)], axis=1),
-            jnp.concatenate([back_in[j, rows:, hs:] for j in range(n)], axis=1),
-        ],
-        axis=0,
-    )
+        heads4[i] = acc[i].astype(BF)
+
+    for j in range(local):
+        mine = slice(j * hs, (j + 1) * hs)
+        keys, values = heads4[1, :, mine], heads4[2, :, mine]
+        slot = j % 2
+        for i in range(n):
+            here = slice(i * rows, (i + 1) * rows)
+            query, grad = heads4[0, here, mine], heads4[3, here, mine]
+            allowed = (
+                jnp.concatenate([jnp.full((rows, TILE), mask[i, t], jnp.int32) for t in range(n)], axis=1)
+                == 1
+            )
+            score = dot(query, keys, 1, 1) * scale
+            weight = jnp.where(allowed, jnp.exp(jnp.where(allowed, score, 0.0)), 0.0)
+            inverse = 1.0 / jnp.sum(weight, -1, keepdims=True)
+            att32 = dot(weight.astype(BF), values, 1, 0) * inverse
+            delta = jnp.sum(grad.astype(F32) * att32, -1, keepdims=True)
+            prob = weight * inverse
+            dprob = dot(grad, values, 1, 1)
+            dscore = (prob * (dprob - delta) * scale).astype(BF)
+            probs[slot, here] = prob.astype(BF)
+            dscores[slot, here] = dscore
+            grads[here, 3 * wide + j * hs : 3 * wide + (j + 1) * hs] = att32.astype(BF)
+            grads[here, mine] = dot(dscore, keys, 1, 0).astype(BF)
+        grads[:, wide + j * hs : wide + (j + 1) * hs] = dot(
+            dscores[slot], heads4[0, :, mine], 0, 0
+        ).astype(BF)
+        grads[:, 2 * wide + j * hs : 2 * wide + (j + 1) * hs] = dot(
+            probs[slot], heads4[3, :, mine], 0, 0
+        ).astype(BF)
+
+    own_rows = pl.ds(pl.multiple_of(b * rows, rows), rows)
+    grad_q = grads[own_rows, :wide]
+    grad_k = grads[own_rows, wide : 2 * wide]
+    grad_v = grads[own_rows, 2 * wide : 3 * wide]
 
     def branch(c):
         cols = pl.ds(pl.multiple_of(c * wide, wide), wide)
@@ -396,6 +359,16 @@
     for k, (c, where) in enumerate(((hx, at_x), (hd, at_d), (hc, at_c))):
         part_out[k] = branch(c).astype(BF)
         sent.append(send(part_out.at[k], part_in.at[k], ps.at[k], pr.at[k], where))
+    three = dot(mixed[b], grads[:, : 3 * wide], 0, 0) * norm
+    for i in range(3):
+        held[i] = three[:, i * wide : (i + 1) * wide]
+    held[3] = dot(slabs[:, b, 1].reshape(n * rows, wide), grads[:, 3 * wide :], 0, 0) * norm
+    writes = [
+        pltpu.make_async_copy(held.at[i], out, sem_w.at[i])
+        for i, out in enumerate((out_q, out_k, out_v, out_o))
+    ]
+    for c in writes:
+        c.start()
     total = branch(h) + slabs[b, h, 1].astype(F32)
     for k in range(3):
         got(part_in.at[k], pr.at[k])
@@ -420,12 +393,6 @@
     edge_in[b] = edge_out[...]
 
     for p in peers:
-        got(wide_in.at[p], gr.at[p])
-    for slot, side, out in ((0, 0, out_q), (0, 1, out_k), (1, 0, out_v), (1, 1, out_o)):
-        out[...] = jnp.concatenate(
-            [wide_in[j, slot, :, side * hs : (side + 1) * hs] for j in range(n)], axis=1
-        ).astype(F32)
-    for p in peers:
         got(edge_in.at[p], er.at[p])
     summed = edge_in[0]
     for j in range(1, n):
@@ -439,6 +406,21 @@
     out_in[...] = total * (1.0 + t[1:2]) + t[0:1] * after + t[2:3] * before
     for c in sent:
         c.wait_send()
+    for c in writes:
+        c.wait()
+
+
+def placed(*refs):
+    ins, outs, held, sems = refs[:6], refs[6:12], refs[12:18], refs[18]
+    loads = [pltpu.make_async_copy(ins[i], held[i], sems.at[0, i]) for i in range(6)]
+    stores = [pltpu.make_async_copy(held[i], outs[i], sems.at[1, i]) for i in range(6)]
+    for c in loads:
+        c.start()
+    for load, store in zip(loads, stores):
+        load.wait()
+        store.start()
+    for c in stores:
+        c.wait()
 
 
 def fused_device(patches, conv_taps, w_query, w_key, w_value, w_output, tile_mask, cotangent):
@@ -447,17 +429,20 @@
     hs = D // HEADS
     tokens = n * rows
     dma = pltpu.SemaphoreType.DMA
-    anywhere = pl.BlockSpec(memory_space=pl.ANY)
-    return pl.pallas_call(
+    anywhere = pl.BlockSpec(memory_space=pltpu.HBM)
+    vmem = pl.BlockSpec(memory_space=pltpu.VMEM)
+    square = jax.ShapeDtypeStruct((D // n, wide), F32)
+    shapes = (
+        jax.ShapeDtypeStruct((rows, wide), F32),
+        jax.ShapeDtypeStruct((3, wide), F32),
+    ) + (square,) * 4
+    results = pl.pallas_call(
         functools.partial(fused, n, tokens ** (-0.5)),
-        out_shape=(
-            jax.ShapeDtypeStruct((rows, wide), F32),
-            jax.ShapeDtypeStruct((3, wide), F32),
-        )
-        + (jax.ShapeDtypeStruct((D // n, wide), F32),) * 4,
-        in_specs=[anywhere] * 6 + [pl.BlockSpec(memory_space=pltpu.SMEM), anywhere],
-        out_specs=(pl.BlockSpec(memory_space=pltpu.VMEM),) * 6,
+        out_shape=shapes,
+        in_specs=[anywhere] * 8,
+        out_specs=(vmem, vmem) + (anywhere,) * 4,
         scratch_shapes=[
+            pltpu.SMEM((n, n), jnp.int32),
             pltpu.VMEM((n, 4, 2, rows, wide), BF),
             pltpu.VMEM((4, tokens, wide), BF),
             pltpu.VMEM((D, wide), BF),
@@ -465,33 +450,35 @@
             pltpu.VMEM((D, wide), BF),
             pltpu.VMEM((D, wide), BF),
             pltpu.VMEM((3, D), F32),
-            pltpu.VMEM((4, tokens, wide // 2), F32),
-            pltpu.VMEM((4, tokens, hs), BF),
-            pltpu.VMEM((tokens, 3 * hs), BF),
-            pltpu.VMEM((tokens, hs), BF),
-            pltpu.VMEM((tokens, hs), F32),
-            pltpu.VMEM((tokens, hs), F32),
-            pltpu.VMEM((n - 1, rows + rows // 2, 2 * hs), BF),
-            pltpu.VMEM((n, rows + rows // 2, 2 * hs), BF),
-            pltpu.VMEM((n - 1, 2, D // n, 2 * hs), BF),
-            pltpu.VMEM((n, 2, D // n, 2 * hs), BF),
+            pltpu.VMEM((4, tokens, wide), F32),
+            pltpu.VMEM((4, tokens, wide), BF),
+            pltpu.VMEM((tokens, 4 * wide), BF),
+            pltpu.VMEM((2, tokens, tokens), BF),
+            pltpu.VMEM((2, tokens, tokens), BF),
+            pltpu.VMEM((4, D // n, wide), F32),
             pltpu.VMEM((3, rows, wide), BF),
             pltpu.VMEM((3, rows, wide), BF),
             pltpu.VMEM((8, wide), F32),
             pltpu.VMEM((n, 8, wide), F32),
-            dma((6,)), dma((4,)),
+            dma((8,)), dma((4,)),
             dma((2, n - 1)), dma((2, n)),
             dma((n,)), dma((n,)),
             dma((2, n)), dma((2, n)),
-            dma((n - 1,)), dma((n,)),
-            dma((n - 1,)), dma((n,)),
             dma((3,)), dma((3,)),
             dma((n - 1,)), dma((n,)),
         ],
         compiler_params=pltpu.CompilerParams(
-            collective_id=0, has_side_effects=True, vmem_limit_bytes=48 * 1024 * 1024
+            collective_id=0, has_side_effects=True, vmem_limit_bytes=60 * 1024 * 1024
         ),
     )(patches, conv_taps, w_query, w_key, w_value, w_output, tile_mask, cotangent)
+    return pl.pallas_call(
+        placed,
+        out_shape=shapes,
+        in_specs=[anywhere] * 6,
+        out_specs=(anywhere,) * 6,
+        scratch_shapes=[pltpu.VMEM(t.shape, F32) for t in shapes] + [dma((2, 6))],
+        compiler_params=pltpu.CompilerParams(vmem_limit_bytes=60 * 1024 * 1024),
+    )(*results)
 
 
 def fits(mesh):

time: 63.6 us -> 50.3 us (0.79)
  local copies, waits for them, and re-layouts: 11.4 us -> 0 us
  Pallas kernels: 51 us -> 49.5 us
    unnamed x22 -> x0, local copies, waits for them, and re-layouts: 11.4 us -> none
    pallas_call x1 -> x2, Pallas kernels: 51 us -> 49.5 us  [the longest x1 47.4 us: fused_device(): pl.pallas_call(functools.partial(fused, n, tokens ** (-0.5)), out_shape=s...]
where the time goes in v2:
time: 50.3 us; the launch traced here: 50.2 us
  Pallas kernels  49.5 us (98%)
  between operations  0.64 us (1%)
    pallas_call x1, Pallas kernels, fused_device(): pl.pallas_call(functools.partial(fused, n, tokens ** (-0.5)), out_shape=s...  47.4 us
    pallas_call x1, Pallas kernels, fused_device(): pl.pallas_call(placed, out_shape=shapes, in_specs=[anywhere] * 6, out_spe...  2.09 us

profile of v2, /device:TPU:0, one launch (start us, length us, event | category | flops | bytes accessed | tf_op | source)
XLA Modules:
  0.0 50.2 jit_solution(13994579489758969761)
XLA Ops:
  0.6 47.4 %shard_map.127 = (f32[128,256]{1,0:T(8,128)}, f32[3,256]{1,0:T(4,128)}, f32[256,256]{1,0:T(8,128)}, f32[256,256]{1,0:T(8,128)}, f32[256,256]{1,0:T(8,128)}, /*index=5*/f32[256,256]{1,0:T(8,128)}) custom-call(bf16[128,1024]{1,0:T(8,128)(2,1)} %patches.1, f32[3,1024]{1,0:T(4,128)} %taps.1, bf16[1024,256]{1,0:T(8,128)(2,1)} %w_query.1, ...), custom_call_target="tpu_custom_call" | custom-call | tf_op jit(solution)/shard_map/pallas_call | solution.py:439
  48.1 2.1 %shard_map.128 = (f32[128,256]{1,0:T(8,128)}, f32[3,256]{1,0:T(4,128)}, f32[256,256]{1,0:T(8,128)}, f32[256,256]{1,0:T(8,128)}, f32[256,256]{1,0:T(8,128)}, /*index=5*/f32[256,256]{1,0:T(8,128)}) custom-call(f32[128,256]{1,0:T(8,128)} %get-tuple-element.12.refs_0_, f32[3,256]{1,0:T(4,128)} %get-tuple-element.13.refs_1_, ...), custom_call_target="tpu_custom_call" | custom-call | tf_op jit(solution)/shard_map/pallas_call | solution.py:474

commit v3 on v2

--- a/solution.py
+++ b/solution.py
@@ -263,18 +263,63 @@
         pl.semaphore_signal(barrier, inc=1, device_id=where, device_id_type=MESH)
     pl.semaphore_wait(barrier, n + 2)
 
-    sent = []
+    sent, relays = [], []
     own_cols = pl.ds(pl.multiple_of(h * wide, wide), wide)
-    for k, where in enumerate(at_peer):
-        sent.append(send(patches.at[:, own_cols], slabs.at[b, h, 0], zs.at[0, k], zr.at[0, b], where))
-        sent.append(send(cot, slabs.at[b, h, 1], zs.at[1, k], zr.at[1, b], where))
-    sent.append(send(cot, slabs.at[b, h, 1], xs.at[0], xr.at[b], at_x))
-    sent.append(send(cot, slabs.at[b, h, 1], cs.at[0, 0], cr.at[0, b], at_c))
-    for k, p in enumerate(peers):
-        got(slabs.at[p, h, 0], zr.at[0, p])
-        got(slabs.at[p, h, 1], zr.at[1, p])
-        sent.append(send(slabs.at[p, h], slabs.at[p, h], xs.at[k + 1], xr.at[p], at_x))
-        sent.append(send(slabs.at[p, h], slabs.at[p, h], cs.at[0, k + 1], cr.at[0, p], at_c))
+    middle = lax.rem((b + 1) // 2, 2)
+    inner, outer, across = b + 1 - 2 * (b // 2), middle * 3 * (b - 1), lax.rem(b + 2, n)
+    last = 3 * (1 - lax.rem(b, 2))
+    order = [
+        inner,
+        middle * last + (1 - middle) * across,
+        middle * across + (1 - middle) * last,
+    ]
+    own_parts = (patches.at[:, own_cols], cot)
+
+    def relay(src, t, kind, k, where):
+        c = pltpu.make_async_remote_copy(
+            src_ref=src, dst_ref=slabs.at[t, h, kind], send_sem=zs.at[kind, k],
+            recv_sem=zr.at[kind, t], device_id=where, device_id_type=MESH,
+        )
+        pl.when(middle == 1)(c.start)
+        relays.append(c)
+
+    at_inner, at_outer = (g, inner, x, s), (g, outer, x, s)
+    for kind in (1, 0):
+        sent.append(
+            send(own_parts[kind], slabs.at[b, h, kind], zs.at[kind, 0], zr.at[kind, b], at_inner)
+        )
+        relay(own_parts[kind], b, kind, 1, at_outer)
+        if kind == 1:
+            sent.append(send(cot, slabs.at[b, h, 1], xs.at[1, 0], xr.at[1, b], at_x))
+            sent.append(send(cot, slabs.at[b, h, 1], cs.at[0, 1, 0], cr.at[0, 1, b], at_c))
+
+    def from_z(k):
+        p = order[k]
+        for kind in (1, 0):
+            part = slabs.at[p, h, kind]
+            got(part, zr.at[kind, p])
+            relay(part, p, kind, k + 2, at_inner if k == 1 else at_outer)
+            sent.append(send(part, part, xs.at[kind, k + 1], xr.at[kind, p], at_x))
+            sent.append(send(part, part, cs.at[0, kind, k + 1], cr.at[0, kind, p], at_c))
+
+    def from_x(k):
+        p = order[k] if k >= 0 else b
+        for kind in (1, 0) if k >= 0 else (1,):
+            part = slabs.at[p, hx, kind]
+            got(part, xr.at[kind, p])
+            sent.append(send(part, part, cs.at[1, kind, k + 1], cr.at[1, kind, p], at_c))
+
+    def from_core(i, c):
+        got(slabs.at[b, c, 1], cr.at[i, 1, b])
+        for p in order:
+            for kind in (1, 0):
+                got(slabs.at[p, c, kind], cr.at[i, kind, p])
+
+    from_z(0)
+    from_x(-1)
+    from_z(1)
+    from_x(0)
+    from_z(2)
     for c in locals_ + weights:
         c.wait()
 
@@ -296,19 +341,12 @@
         acc[3] += dot(cq, wo[cols, :], 1, 0)
 
     quarter(h)
-    got(slabs.at[b, hx, 1], xr.at[b])
-    sent.append(send(slabs.at[b, hx, 1], slabs.at[b, hx, 1], cs.at[1, 0], cr.at[1, b], at_c))
-    for k, p in enumerate(peers):
-        got(slabs.at[p, hx], xr.at[p])
-        sent.append(send(slabs.at[p, hx], slabs.at[p, hx], cs.at[1, k + 1], cr.at[1, p], at_c))
+    from_x(1)
+    from_x(2)
+    from_core(0, hc)
+    quarter(hc)
     quarter(hx)
-    got(slabs.at[b, hc, 1], cr.at[0, b])
-    for p in peers:
-        got(slabs.at[p, hc], cr.at[0, p])
-    quarter(hc)
-    got(slabs.at[b, hd, 1], cr.at[1, b])
-    for p in peers:
-        got(slabs.at[p, hd], cr.at[1, p])
+    from_core(1, hd)
     quarter(hd)
 
     for i in range(4):
@@ -406,6 +444,8 @@
     out_in[...] = total * (1.0 + t[1:2]) + t[0:1] * after + t[2:3] * before
     for c in sent:
         c.wait_send()
+    for c in relays:
+        pl.when(middle == 1)(c.wait_send)
     for c in writes:
         c.wait()
 
@@ -461,9 +501,9 @@
             pltpu.VMEM((8, wide), F32),
             pltpu.VMEM((n, 8, wide), F32),
             dma((8,)), dma((4,)),
-            dma((2, n - 1)), dma((2, n)),
-            dma((n,)), dma((n,)),
+            dma((2, n + 1)), dma((2, n)),
             dma((2, n)), dma((2, n)),
+            dma((2, 2, n)), dma((2, 2, n)),
             dma((3,)), dma((3,)),
             dma((n - 1,)), dma((n,)),
         ],

time: 50.3 us -> 45.2 us (0.90)
  Pallas kernels: 49.5 us -> 44.4 us
    pallas_call x1, Pallas kernels: 47.4 us -> 42.4 us  [fused_device(): pl.pallas_call(functools.partial(fused, n, tokens ** (-0.5)), out_shape=s...]
where the time goes in v3:
time: 45.2 us; the launch traced here: 45.1 us
  Pallas kernels  44.4 us (98%)
  between operations  0.64 us (1%)
    pallas_call x1, Pallas kernels, fused_device(): pl.pallas_call(functools.partial(fused, n, tokens ** (-0.5)), out_shape=s...  42.4 us
    pallas_call x1, Pallas kernels, fused_device(): pl.pallas_call(placed, out_shape=shapes, in_specs=[anywhere] * 6, out_spe...  2.09 us

profile of v3, /device:TPU:0, one launch (start us, length us, event | category | flops | bytes accessed | tf_op | source)
XLA Modules:
  0.0 45.1 jit_solution(12939328942011057523)
XLA Ops:
  0.6 42.4 %shard_map.127 = (f32[128,256]{1,0:T(8,128)}, f32[3,256]{1,0:T(4,128)}, f32[256,256]{1,0:T(8,128)}, f32[256,256]{1,0:T(8,128)}, f32[256,256]{1,0:T(8,128)}, /*index=5*/f32[256,256]{1,0:T(8,128)}) custom-call(bf16[128,1024]{1,0:T(8,128)(2,1)} %patches.1, f32[3,1024]{1,0:T(4,128)} %taps.1, bf16[1024,256]{1,0:T(8,128)(2,1)} %w_query.1, ...), custom_call_target="tpu_custom_call" | custom-call | tf_op jit(solution)/shard_map/pallas_call | solution.py:479
  43.0 2.1 %shard_map.128 = (f32[128,256]{1,0:T(8,128)}, f32[3,256]{1,0:T(4,128)}, f32[256,256]{1,0:T(8,128)}, f32[256,256]{1,0:T(8,128)}, f32[256,256]{1,0:T(8,128)}, /*index=5*/f32[256,256]{1,0:T(8,128)}) custom-call(f32[128,256]{1,0:T(8,128)} %get-tuple-element.12.refs_0_, f32[3,256]{1,0:T(4,128)} %get-tuple-element.13.refs_1_, ...), custom_call_target="tpu_custom_call" | custom-call | tf_op jit(solution)/shard_map/pallas_call | solution.py:514

commit v4 on v3

--- a/solution.py
+++ b/solution.py
@@ -212,7 +212,7 @@
     n, norm,
     patches, taps, w_query, w_key, w_value, w_output, mask_in, cot,
     out_in, out_conv, out_q, out_k, out_v, out_o,
-    mask, slabs, mixed, wq, wk, wv, wo, tp, acc, heads4, grads, probs, dscores, held,
+    mask, slabs, mixed, wq, wk, wv, wo, tp, acc, heads4, grads, plane, probs, dscores, held,
     part_out, part_in, edge_out, edge_in,
     sem_loc, sem_w, zs, zr, xs, xr, cs, cr, ps, pr, es, er,
 ):
@@ -354,27 +354,31 @@
 
     for j in range(local):
         mine = slice(j * hs, (j + 1) * hs)
-        keys, values = heads4[1, :, mine], heads4[2, :, mine]
+        queries, keys, values, grad = (heads4[i, :, mine] for i in (0, 1, 2, 3))
         slot = j % 2
+        plane[slot, 0] = dot(queries, keys, 1, 1)
+        plane[slot, 1] = dot(grad, values, 1, 1)
+        inverses = []
         for i in range(n):
             here = slice(i * rows, (i + 1) * rows)
-            query, grad = heads4[0, here, mine], heads4[3, here, mine]
             allowed = (
                 jnp.concatenate([jnp.full((rows, TILE), mask[i, t], jnp.int32) for t in range(n)], axis=1)
                 == 1
             )
-            score = dot(query, keys, 1, 1) * scale
+            score = plane[slot, 0, here] * scale
             weight = jnp.where(allowed, jnp.exp(jnp.where(allowed, score, 0.0)), 0.0)
-            inverse = 1.0 / jnp.sum(weight, -1, keepdims=True)
-            att32 = dot(weight.astype(BF), values, 1, 0) * inverse
-            delta = jnp.sum(grad.astype(F32) * att32, -1, keepdims=True)
-            prob = weight * inverse
-            dprob = dot(grad, values, 1, 1)
-            dscore = (prob * (dprob - delta) * scale).astype(BF)
+            inverses.append(1.0 / jnp.sum(weight, -1, keepdims=True))
+            plane[slot, 0, here] = weight
+            probs[slot, here] = weight.astype(BF)
+        att32 = dot(probs[slot], values, 1, 0) * jnp.concatenate(inverses, axis=0)
+        grads[:, 3 * wide + j * hs : 3 * wide + (j + 1) * hs] = att32.astype(BF)
+        delta = jnp.sum(grad.astype(F32) * att32, -1, keepdims=True)
+        for i in range(n):
+            here = slice(i * rows, (i + 1) * rows)
+            prob = plane[slot, 0, here] * inverses[i]
             probs[slot, here] = prob.astype(BF)
-            dscores[slot, here] = dscore
-            grads[here, 3 * wide + j * hs : 3 * wide + (j + 1) * hs] = att32.astype(BF)
-            grads[here, mine] = dot(dscore, keys, 1, 0).astype(BF)
+            dscores[slot, here] = (prob * (plane[slot, 1, here] - delta[here]) * scale).astype(BF)
+        grads[:, mine] = dot(dscores[slot], keys, 1, 0).astype(BF)
         grads[:, wide + j * hs : wide + (j + 1) * hs] = dot(
             dscores[slot], heads4[0, :, mine], 0, 0
         ).astype(BF)
@@ -493,6 +497,7 @@
             pltpu.VMEM((4, tokens, wide), F32),
             pltpu.VMEM((4, tokens, wide), BF),
             pltpu.VMEM((tokens, 4 * wide), BF),
+            pltpu.VMEM((2, 2, tokens, tokens), F32),
             pltpu.VMEM((2, tokens, tokens), BF),
             pltpu.VMEM((2, tokens, tokens), BF),
             pltpu.VMEM((4, D // n, wide), F32),

time: 45.2 us -> 43.4 us (0.960)
  Pallas kernels: 44.4 us -> 42.6 us
    pallas_call x1, Pallas kernels: 42.4 us -> 40.5 us  [fused_device(): pl.pallas_call(functools.partial(fused, n, tokens ** (-0.5)), out_shape=s...]
where the time goes in v4:
time: 43.4 us; the launch traced here: 43.2 us
  Pallas kernels  42.6 us (98%)
  between operations  0.64 us (1%)
    pallas_call x1, Pallas kernels, fused_device(): pl.pallas_call(functools.partial(fused, n, tokens ** (-0.5)), out_shape=s...  40.5 us
    pallas_call x1, Pallas kernels, fused_device(): pl.pallas_call(placed, out_shape=shapes, in_specs=[anywhere] * 6, out_spe...  2.09 us

profile of v4, /device:TPU:0, one launch (start us, length us, event | category | flops | bytes accessed | tf_op | source)
XLA Modules:
  0.0 43.2 jit_solution(5170959513928493802)
XLA Ops:
  0.6 40.5 %shard_map.127 = (f32[128,256]{1,0:T(8,128)}, f32[3,256]{1,0:T(4,128)}, f32[256,256]{1,0:T(8,128)}, f32[256,256]{1,0:T(8,128)}, f32[256,256]{1,0:T(8,128)}, /*index=5*/f32[256,256]{1,0:T(8,128)}) custom-call(bf16[128,1024]{1,0:T(8,128)(2,1)} %patches.1, f32[3,1024]{1,0:T(4,128)} %taps.1, bf16[1024,256]{1,0:T(8,128)(2,1)} %w_query.1, ...), custom_call_target="tpu_custom_call" | custom-call | tf_op jit(solution)/shard_map/pallas_call | solution.py:483
  41.1 2.1 %shard_map.128 = (f32[128,256]{1,0:T(8,128)}, f32[3,256]{1,0:T(4,128)}, f32[256,256]{1,0:T(8,128)}, f32[256,256]{1,0:T(8,128)}, f32[256,256]{1,0:T(8,128)}, /*index=5*/f32[256,256]{1,0:T(8,128)}) custom-call(f32[128,256]{1,0:T(8,128)} %get-tuple-element.12.refs_0_, f32[3,256]{1,0:T(4,128)} %get-tuple-element.13.refs_1_, ...), custom_call_target="tpu_custom_call" | custom-call | tf_op jit(solution)/shard_map/pallas_call | solution.py:519

commit v5 on v4

--- a/solution.py
+++ b/solution.py
@@ -342,9 +342,9 @@
 
     quarter(h)
     from_x(1)
-    from_x(2)
     from_core(0, hc)
     quarter(hc)
+    from_x(2)
     quarter(hx)
     from_core(1, hd)
     quarter(hd)

time: 43.4 us -> 43.4 us (level)
  no operation moved by 1% of the time
where the time goes in v5:
time: 43.4 us; the launch traced here: 43.2 us
  Pallas kernels  42.6 us (98%)
  between operations  0.64 us (1%)
    pallas_call x1, Pallas kernels, fused_device(): pl.pallas_call(functools.partial(fused, n, tokens ** (-0.5)), out_shape=s...  40.5 us
    pallas_call x1, Pallas kernels, fused_device(): pl.pallas_call(placed, out_shape=shapes, in_specs=[anywhere] * 6, out_spe...  2.09 us

profile of v5, /device:TPU:0, one launch (start us, length us, event | category | flops | bytes accessed | tf_op | source)
XLA Modules:
  0.0 43.2 jit_solution(15432276147823781261)
XLA Ops:
  0.6 40.5 %shard_map.127 = (f32[128,256]{1,0:T(8,128)}, f32[3,256]{1,0:T(4,128)}, f32[256,256]{1,0:T(8,128)}, f32[256,256]{1,0:T(8,128)}, f32[256,256]{1,0:T(8,128)}, /*index=5*/f32[256,256]{1,0:T(8,128)}) custom-call(bf16[128,1024]{1,0:T(8,128)(2,1)} %patches.1, f32[3,1024]{1,0:T(4,128)} %taps.1, bf16[1024,256]{1,0:T(8,128)(2,1)} %w_query.1, ...), custom_call_target="tpu_custom_call" | custom-call | tf_op jit(solution)/shard_map/pallas_call | solution.py:483
  41.1 2.1 %shard_map.128 = (f32[128,256]{1,0:T(8,128)}, f32[3,256]{1,0:T(4,128)}, f32[256,256]{1,0:T(8,128)}, f32[256,256]{1,0:T(8,128)}, f32[256,256]{1,0:T(8,128)}, /*index=5*/f32[256,256]{1,0:T(8,128)}) custom-call(f32[128,256]{1,0:T(8,128)} %get-tuple-element.12.refs_0_, f32[3,256]{1,0:T(4,128)} %get-tuple-element.13.refs_1_, ...), custom_call_target="tpu_custom_call" | custom-call | tf_op jit(solution)/shard_map/pallas_call | solution.py:519
